TPU v7x, 32 devices: a whole 2x2x4 slice. The times are simulated.
32 devices in a mesh: rows: 16 (over z, x, core), heads: 2 (over y).
Axes of the slice: x: 2, y: 2, z: 4, core: 2. Of those that a mesh axis runs over, the one named last changes fastest.
Arguments:
- hidden: bfloat16 [2, 16, 8192], P(None, None, 'rows'), may hold values from -6 to 6
- norm_gain: bfloat16 [8192], P('rows'), may hold values from 0.5 to 2
- query_weight: bfloat16 [8192, 8192], P('rows', 'heads'), may hold values from -0.0625 to 0.0625
- query_gain: bfloat16 [128], replicated, may hold values from 0.5 to 2
- out_weight: bfloat16 [8192, 8192], P('heads', 'rows'), may hold values from -0.0625 to 0.0625
- attn_gate: float32 [1], replicated, may hold values from 0.3 to 1.5
- kv_cache: bfloat16 [16, 8, 4, 1408, 256], P('rows', 'heads'), may hold values from -384 to 384
- new_tiles: bfloat16 [16, 8, 1408, 256], P('rows', 'heads'), may hold values from -384 to 384
- counts: int32 [2, 16], P(None, 'rows'), may hold values from 1 to 4, as said below
- join_list: int32 [2, 2, 3], replicated, may hold values from 0 to 15, as said below
Outputs:
- mixed: bfloat16 [2, 16, 8192], P(None, None, 'rows')
- arrived: bfloat16 [16, 8, 1408, 256], P('rows', 'heads')
Inputs may be any that keep to these rules, and one draw needn't show every extreme that they name: Some row has 4 tiles and some row one tile at each step; a row that receives a tile in slot k at some step counts more than k tiles at that step and every later one. `join_list`: sources are distinct over all entries, below 16; targets are distinct over all entries, below 16; slots are below 4.
All inputs are finite; a program needn't handle non-finite values.
Results may differ from a plain program's by a relative error of at most 0.0045.
The roundings to bfloat16 on the way count: a program that leaves them out, or rounds other values in their place, can miss the bound.
Values may be sent and summed in bfloat16 or wider, within the bound.
No kernel may reach another device: no remote copies, remote signals or barrier semaphores. Data moves between devices by JAX's collectives and lax.ppermute only.
A program may use at most 128 MiB of HBM per device.

v0:
```python
import functools
import math

import jax
import jax.numpy as jnp
from jax import lax
from jax.experimental import pallas as pl
from jax.experimental.pallas import tpu as pltpu
from jax.sharding import PartitionSpec as P

STEPS = 2
JOINS = 2
TOTAL = STEPS * JOINS

epsilon = 1e-05

ROUNDS = [(0, 0, 0, 0), (0, 1, 0, 0), (0, 0, 1, 0), (0, 0, 0, 1),
          (0, 1, 1, 0), (0, 1, 0, 1), (0, 0, 1, 1), (0, 1, 1, 1)]


def write_plan(rows, join_ref, only_ref, way_ref, plan_ref):
    me = lax.axis_index("rows")
    source, target, slot = [], [], []
    for s in range(STEPS):
        for j in range(JOINS):
            source.append(join_ref[s, j, 0])
            target.append(join_ref[s, j, 1])
            slot.append(join_ref[s, j, 2])
    one, zero = jnp.int32(1), jnp.int32(0)

    busy = []
    for i in range(TOTAL):
        for sender in (source[i], source[i] ^ 1):
            hit = zero
            for j in range(TOTAL):
                if j != i:
                    hit = hit | jnp.where(sender == target[j], one, zero)
            busy.append(hit)
    same = {}
    for i in range(TOTAL):
        for j in range(i + 1, TOTAL):
            same[i, j] = jnp.where(source[i] == (source[j] ^ 1), one, zero)
    single = zero
    swap = [zero] * TOTAL
    choices = sorted(range(2 ** TOTAL), key=lambda m: (-bin(m).count("1"), m))
    for m in choices:
        bits = [(m >> i) & 1 for i in range(TOTAL)]
        bad = zero
        for i in range(TOTAL):
            bad = bad | busy[2 * i + bits[i]]
        for (i, j), value in same.items():
            if bits[i] != bits[j]:
                bad = bad | value
        good = bad == 0
        single = jnp.where(good, one, single)
        swap = [jnp.where(good, jnp.int32(b), w) for b, w in zip(bits, swap)]

    clash = {}
    for i in range(TOTAL):
        for j in range(i + 1, TOTAL):
            both = (source[i] == target[j]) | (source[j] == target[i])
            clash[i, j] = jnp.where(both, one, zero)
    best = [zero] * TOTAL
    double = zero
    for rounds in reversed(ROUNDS):
        bad = zero
        for (i, j), value in clash.items():
            if rounds[i] == rounds[j]:
                bad = bad | value
        good = bad == 0
        double = jnp.where(good, one, double)
        best = [jnp.where(good, jnp.int32(r), b) for r, b in zip(rounds, best)]

    def kind_of(s, t):
        key = s ^ t
        return jnp.where(key == 0, 1, 2 * key + jnp.where(s < t, 0, 1))

    only, branch = zero, [zero, zero]
    arrives, step, place = zero, jnp.int32(STEPS), zero
    for i in range(TOTAL):
        s, t = source[i], target[i]
        sender = s ^ swap[i]
        part = (me == sender) | (me == t)
        only = jnp.where(part, kind_of(sender, t) + swap[i] * (2 * rows - 1), only)
        part = (me == s) | (me == t)
        for r in range(2):
            branch[r] = jnp.where(part & (best[i] == r), kind_of(s, t), branch[r])
        here = me == t
        arrives = jnp.where(here, best[i] + 1, arrives)
        step = jnp.where(here, i // JOINS, step)
        place = jnp.where(here, slot[i], place)
    only_ref[0] = only
    way_ref[0] = jnp.where(single > 0, 0, jnp.where(double > 0, 1, 2))
    plan_ref[0] = branch[0]
    plan_ref[1] = branch[1]
    plan_ref[2] = arrives
    plan_ref[3] = step
    plan_ref[4] = place
    for i in range(5, 8):
        plan_ref[i] = zero


def project_kernel(
    rows, head_size, join_ref, hidden_ref, gain_ref, weight_ref,
    keep_ref, send_ref, only_ref, way_ref, plan_ref, scaled_ref,
):
    chips = rows // 2

    @pl.when(pl.program_id(0) == 0)
    def _():
        write_plan(rows, join_ref, only_ref, way_ref, plan_ref)
        scaled = hidden_ref[...].astype(jnp.float32) * gain_ref[...].astype(jnp.float32)[None, :]
        scaled = scaled.astype(jnp.bfloat16)
        count = STEPS * rows
        to = lax.broadcasted_iota(jnp.int32, (count, count), 0)
        given = lax.broadcasted_iota(jnp.int32, (count, count), 1)
        core = (to // (STEPS * chips)) ^ (lax.axis_index("rows") & 1)
        wanted = lax.rem(to // chips, STEPS) * rows + lax.rem(to, chips) * 2 + core
        shuffle = jnp.where(given == wanted, 1.0, 0.0).astype(jnp.bfloat16)
        scaled_ref[...] = jnp.dot(
            shuffle, scaled, preferred_element_type=jnp.float32
        ).astype(jnp.bfloat16)

    product = jnp.dot(scaled_ref[...], weight_ref[...], preferred_element_type=jnp.float32)
    for h in range(weight_ref.shape[1] // head_size):
        piece = product[:, h * head_size:(h + 1) * head_size]
        for s in range(STEPS):
            keep_ref[:, s, h, :] = piece[s * chips:(s + 1) * chips]
            start = (STEPS + s) * chips
            send_ref[:, s, h, :] = piece[start:start + chips]


def project(rows, head_size, join_list, hidden, norm_gain, query_weight):
    width, columns = query_weight.shape
    chips = rows // 2
    heads_here = columns // head_size
    parts = 4 if heads_here % 32 == 0 else 1
    smem = pl.BlockSpec(memory_space=pltpu.SMEM)
    block = pl.BlockSpec((chips, STEPS, heads_here // parts, head_size), lambda i: (0, 0, i, 0))
    sums = jax.ShapeDtypeStruct((chips, STEPS, heads_here, head_size), jnp.float32)
    return pl.pallas_call(
        functools.partial(project_kernel, rows, head_size),
        grid=(parts,),
        out_shape=(
            sums,
            sums,
            jax.ShapeDtypeStruct((1,), jnp.int32),
            jax.ShapeDtypeStruct((1,), jnp.int32),
            jax.ShapeDtypeStruct((8,), jnp.int32),
        ),
        in_specs=[
            smem,
            pl.BlockSpec((STEPS * rows, width), lambda i: (0, 0)),
            pl.BlockSpec((width,), lambda i: (0,)),
            pl.BlockSpec((width, columns // parts), lambda i: (0, i)),
        ],
        out_specs=(block, block, smem, smem, smem),
        scratch_shapes=[pltpu.VMEM((STEPS * rows, width), jnp.bfloat16)],
        compiler_params=pltpu.CompilerParams(vmem_limit_bytes=60 * 1024 * 1024),
        cost_estimate=pl.CostEstimate(
            flops=2 * STEPS * rows * width * columns,
            bytes_accessed=2 * width * columns + 4 * STEPS * rows * columns,
            transcendentals=0,
        ),
        name="project",
    )(join_list, hidden.reshape(STEPS * rows, width), norm_gain, query_weight)


def transfer(branch, rows, *tiles):
    branches = [lambda *blocks: jnp.zeros_like(blocks[0])]

    def keep(index):
        return lambda *blocks: blocks[index]

    def send(index, pairs):
        return lambda *blocks: lax.ppermute(blocks[index], "rows", pairs)

    for index in range(len(tiles)):
        branches.append(keep(index))
        for key in range(1, rows):
            for low in (True, False):
                pairs = [(i, i ^ key) for i in range(rows) if (i < (i ^ key)) == low]
                branches.append(send(index, pairs))
    return lax.switch(branch, branches, *tiles)


def move_tiles(only, way, plan, join_list, rows, own, other):
    me = lax.axis_index("rows")

    def once(own, other):
        return transfer(only[0], rows, own, other)

    def twice(own, other):
        first = transfer(plan[0], rows, own)
        second = transfer(plan[1], rows, own)
        late = plan[2] == 2
        return jnp.where(plan[2] == 1, first, jnp.where(late, second, jnp.zeros_like(own)))

    def summed(own, other):
        result = jnp.zeros_like(own)
        for s in range(STEPS):
            for j in range(JOINS):
                given = jnp.where(me == join_list[s, j, 0], own, jnp.zeros_like(own))
                given = lax.psum(given, "rows")
                result = jnp.where(me == join_list[s, j, 1], given, result)
        return result

    return lax.switch(way[0], [once, twice, summed], own, other)


def attend_kernel(
    group, head_size, plan_ref, counts_ref, gain_ref, sums_ref, cache_ref, new_ref,
    out_ref, kept_ref, held, fresh, cache_sem, new_sem, kept_sem,
):
    _, kv_here, slots, _, _ = cache_ref.shape
    join_step, join_slot = plan_ref[3], plan_ref[4]
    one, zero = jnp.int32(1), jnp.int32(0)
    joined = join_step < STEPS

    def shown_at(s, i):
        return (i < counts_ref[s, 0]) & ((join_step > s) | (join_slot != i))

    needed = []
    for i in range(slots):
        any_step = shown_at(0, i)
        for s in range(1, STEPS):
            any_step = any_step | shown_at(s, i)
        needed.append(any_step)

    def fetch(h, i):
        return pltpu.make_async_copy(cache_ref.at[0, h, i], held.at[h, i], cache_sem.at[h, i])

    def fetch_new(h):
        return pltpu.make_async_copy(new_ref.at[h], fresh.at[h], new_sem.at[h])

    def keep(h):
        return pltpu.make_async_copy(fresh.at[h], kept_ref.at[h], kept_sem.at[h])

    for h in range(kv_here):
        for i in range(slots):
            pl.when(needed[i])(fetch(h, i).start)
        pl.when(joined)(fetch_new(h).start)

    @pl.when(jnp.logical_not(joined))
    def _():
        fresh[...] = jnp.zeros_like(fresh)

    step = lax.broadcasted_iota(jnp.int32, (STEPS * group, 1), 0) // group
    raw = sums_ref[0]
    for k in range(1, sums_ref.shape[0]):
        raw = raw + sums_ref[k]
    gain = gain_ref[...].astype(jnp.float32)
    for h in range(kv_here):
        rows = raw[:, h * group:(h + 1) * group].reshape(STEPS * group, head_size)
        queries = (
            rows
            * lax.rsqrt(jnp.mean(rows * rows, axis=-1, keepdims=True) + epsilon)
            * gain
        ).astype(jnp.bfloat16)
        for i in range(slots):
            pl.when(needed[i])(fetch(h, i).wait)
        pl.when(joined)(fetch_new(h).wait)
        keep(h).start()

        def scores_of(keys, shown):
            scores = lax.dot_general(
                queries, keys, (((1,), (1,)), ((), ())), preferred_element_type=jnp.float32
            ) * (1.0 / math.sqrt(head_size))
            usable = jnp.where(step == 1, shown[1], shown[0]) > 0
            return jnp.where(usable, scores, -1e30)

        all_scores = []
        for i in range(slots):
            shown = [jnp.where(shown_at(s, i), one, zero) for s in range(STEPS)]
            all_scores.append(scores_of(held[h, i, :, :head_size], shown))
        shown = [jnp.where(join_step <= s, one, zero) for s in range(STEPS)]
        all_scores.append(scores_of(fresh[h, :, :head_size], shown))
        highest = all_scores[0].max(axis=-1, keepdims=True)
        for scores in all_scores[1:]:
            highest = jnp.maximum(highest, scores.max(axis=-1, keepdims=True))
        exponents = [jnp.exp(scores - highest) for scores in all_scores]
        total = exponents[0].sum(axis=-1, keepdims=True)
        for exponent in exponents[1:]:
            total = total + exponent.sum(axis=-1, keepdims=True)
        context = jnp.zeros((STEPS * group, head_size), jnp.float32)
        for i, exponent in enumerate(exponents):
            probs = (exponent / total).astype(jnp.bfloat16)
            if i < slots:
                values = held[h, i, :, head_size:]
                values = jnp.where(needed[i], values, jnp.zeros_like(values))
            else:
                values = fresh[h, :, head_size:]
            context = context + jnp.dot(probs, values, preferred_element_type=jnp.float32)
        for g in range(group):
            for s in range(STEPS):
                r = s * group + g
                start = (h * group + g) * head_size
                out_ref[s:s + 1, start:start + head_size] = context[r:r + 1]
    for h in range(kv_here):
        keep(h).wait()


def attend(plan, counts, query_gain, sums, kv_cache, arrived):
    _, kv_here, slots, tile_len, width = kv_cache.shape
    _, _, heads_here, head_size = sums.shape
    group = heads_here // kv_here
    smem = pl.BlockSpec(memory_space=pltpu.SMEM)
    vmem = pl.BlockSpec(memory_space=pltpu.VMEM)
    hbm = pl.BlockSpec(memory_space=pl.ANY)
    return pl.pallas_call(
        functools.partial(attend_kernel, group, head_size),
        in_specs=[smem, smem, vmem, vmem, hbm, hbm],
        out_specs=(vmem, hbm),
        out_shape=(
            jax.ShapeDtypeStruct((STEPS, heads_here * head_size), jnp.float32),
            jax.ShapeDtypeStruct(arrived.shape, jnp.bfloat16),
        ),
        scratch_shapes=[
            pltpu.VMEM((kv_here, slots, tile_len, width), jnp.bfloat16),
            pltpu.VMEM((kv_here, tile_len, width), jnp.bfloat16),
            pltpu.SemaphoreType.DMA((kv_here, slots)),
            pltpu.SemaphoreType.DMA((kv_here,)),
            pltpu.SemaphoreType.DMA((kv_here,)),
        ],
        compiler_params=pltpu.CompilerParams(vmem_limit_bytes=53 * 1024 * 1024),
        cost_estimate=pl.CostEstimate(
            flops=4 * kv_here * (slots + 1) * tile_len * width * group,
            bytes_accessed=kv_here * (slots + 2) * tile_len * width * 2,
            transcendentals=kv_here * (slots + 1) * tile_len * group * STEPS,
        ),
        name="attend",
    )(plan, counts, query_gain.reshape(1, head_size), sums, kv_cache, arrived)


def on_device(
    rows,
    heads,
    hidden,
    norm_gain,
    query_weight,
    query_gain,
    out_weight,
    attn_gate,
    kv_cache,
    new_tiles,
    counts,
    join_list,
):
    width = hidden.shape[2]
    me = lax.axis_index("rows")
    odd = (me & 1) > 0
    chips = rows // 2
    own_tile = new_tiles[0]

    def across(block, axis, size, key):
        return lax.ppermute(block, axis, [(i, i ^ key) for i in range(size)])

    same_core = [list(range(core, rows, 2)) for core in range(2)]

    def between_chips(blocks):
        return lax.all_to_all(blocks, "rows", 0, 0, axis_index_groups=same_core, tiled=True)

    other_tile = across(own_tile, "rows", rows, 1)
    head_size = kv_cache.shape[4] // 2
    columns = query_weight.shape[1]
    keep, send, only, way, plan = project(
        rows, head_size, join_list, hidden, norm_gain, query_weight
    )
    sums = between_chips(keep + across(send, "rows", rows, 1))
    arrived = move_tiles(only, way, plan, join_list, rows, own_tile, other_tile)
    context, arrived = attend(plan, counts, query_gain, sums, kv_cache, arrived)
    context = context.astype(jnp.bfloat16)
    mine = between_chips(jnp.broadcast_to(context, (chips, STEPS, columns)))
    theirs = across(mine, "rows", rows, 1)
    gathered = jnp.stack(
        [jnp.where(odd, theirs, mine), jnp.where(odd, mine, theirs)], axis=1
    )
    gathered = gathered.transpose(2, 0, 1, 3).reshape(STEPS * rows, columns)
    projected = jnp.dot(gathered, out_weight, preferred_element_type=jnp.float32)
    key = 1
    while key < heads:
        projected = projected + across(projected, "heads", heads, key)
        key *= 2
    projected = projected.reshape(STEPS, rows, width)
    mixed = (hidden.astype(jnp.float32) + jnp.tanh(attn_gate[0]) * projected).astype(jnp.bfloat16)
    return mixed, arrived[None]


def solution(mesh):
    in_specs = (
        P(None, None, "rows"),
        P("rows"),
        P("rows", "heads"),
        P(),
        P("heads", "rows"),
        P(),
        P("rows", "heads", None, None, None),
        P("rows", "heads", None, None),
        P(None, "rows"),
        P(),
    )
    out_specs = (P(None, None, "rows"), P("rows", "heads", None, None))
    body = functools.partial(on_device, mesh.shape["rows"], mesh.shape["heads"])
    return jax.shard_map(
        body, mesh=mesh, in_specs=in_specs, out_specs=out_specs, check_vma=False
    )
```

profile of v0, /device:TPU:0, one launch (start us, length us, event | category | flops | bytes accessed | tf_op | source)
XLA Modules:
  0.0 100.0 jit_solution(6029492996769666168)
XLA Ops:
  7.2 0.5 collective-permute-start.121
  7.7 5.1 %project.1 = (f32[8,2,32,128]{3,2,1,0:T(8,128)}, f32[8,2,32,128]{3,2,1,0:T(8,128)}, s32[1]{0:T(128)}, s32[1]{0:T(128)}, s32[8]{0:T(128)S(1)}) custom-call(s32[2,2,3]{2,1,0:T(2,128)} %join_ref.1, bf16[32,512]{1,0:T(8,128)(2,1)} %bitcast.34, bf16[512]{0:T(512)(128)(2,1)} %gain_ref.1, bf16[512,4096]{1,0:T(8,128)(2,1)} %weight_ref.1), custom_call_target="tpu_custom_call" | custom-call | flops 134217728 | bytes 4718592 | tf_op jit(solution)/shard_map/project/pallas_call | solution.py:141
  12.8 1.7 %collective-permute-done.120 = f32[8,2,32,128]{3,2,1,0:T(8,128)S(1)} collective-permute-done((f32[8,2,32,128]{3,2,1,0:T(8,128)}, f32[8,2,32,128]{3,2,1,0:T(8,128)S(1)}, u32[]{:S(2)}, u32[]{:S(2)}) %collective-permute-start.120) | collective-permute-done | bytes 262176 | tf_op jit(solution)/shard_map/ppermute | solution.py:356
  14.5 1.7 %add.17 = f32[8,2,32,128]{3,2,1,0:T(8,128)} add(f32[8,2,32,128]{3,2,1,0:T(8,128)} %get-tuple-element.292, f32[8,2,32,128]{3,2,1,0:T(8,128)S(1)} %collective-permute-done.120) | non-fusion elementwise | flops 65536 | bytes 786432 | tf_op jit(solution)/shard_map/add | solution.py:369
  16.2 6.8 %all-to-all-start = ((f32[8,2,32,128]{3,2,1,0:T(8,128)}), f32[8,2,32,128]{3,2,1,0:T(8,128)S(1)}, u32[]{:S(2)}, u32[]{:S(2)}) async-start(f32[8,2,32,128]{3,2,1,0:T(8,128)} %add.17), calls=%async_computation | async-start | bytes 524288 | tf_op jit(solution)/shard_map/all_to_all | solution.py:361
  23.0 0.1 copy.17.counts_ref
  23.8 0.0 copy-start
  23.8 2.5 %conditional.4 = (bf16[4,1408,256]{2,1,0:T(8,128)(2,1)}) conditional(s32[]{:T(128)} %bitcast.16, (s32[1]{0:T(128)}, bf16[4,1408,256]{2,1,0:T(8,128)(2,1)S(1)}, bf16[4,1408,256]{2,1,0:T(8,128)(2,1)}) %tuple.548, (s32[8]{0:T(128)S(1)}, bf16[4,1408,256]{2,1,0:T(8,128)(2,1)S(1)}) %tuple.549, (s32[2,2,3]{2,1,0:T(2,128)S(1)}, ...), branch_computations={%region_0.0_spmd, %region_64.129_spmd, %region_129.134_spmd} | conditional | flops 17301512 | bytes 98042040 | solution.py:208
  24.4 1.8 %conditional = (bf16[4,1408,256]{2,1,0:T(8,128)(2,1)}) conditional(s32[]{:T(128)} %bitcast, () %tuple.390, bf16[4,1408,256]{2,1,0:T(8,128)(2,1)S(1)} %get-tuple-element.271, bf16[4,1408,256]{2,1,0:T(8,128)(2,1)S(1)} %get-tuple-element.271, bf16[4,1408,256]{2,1,0:T(8,128)(2,1)S(1)} %get-tuple-element.271, ...), branch_computations={%region_1.0_spmd, %region_2.0_spmd, %region_3.0_spmd, %region_4.0_... | conditional | bytes 11534384 | solution.py:184
  24.5 1.8 %broadcast.12 = bf16[4,1408,256]{2,1,0:T(8,128)(2,1)} broadcast(bf16[]{:T(256)} %constant.15.clone), dimensions={} | broadcast | bytes 2883586 | tf_op jit(solution)/shard_map/broadcast.1
  26.2 6.2 %all-to-all-done.sums_ref = f32[8,2,32,128]{3,2,1,0:T(8,128)S(1)} async-done(((f32[8,2,32,128]{3,2,1,0:T(8,128)}), f32[8,2,32,128]{3,2,1,0:T(8,128)S(1)}, u32[]{:S(2)}, u32[]{:S(2)}) %all-to-all-start) | async-done | bytes 262176 | tf_op jit(solution)/shard_map/all_to_all | solution.py:361
  32.4 6.8 %attend.1 = (f32[2,4096]{1,0:T(2,128)S(1)}, bf16[4,1408,256]{2,1,0:T(8,128)(2,1)}) custom-call(s32[8]{0:T(128)S(1)} %get-tuple-element.291.plan_ref, s32[2,1]{1,0:T(2,128)S(1)} %copy.17.counts_ref, bf16[1,128]{1,0:T(2,128)(2,1)S(1)} %bitcast.28, f32[8,2,32,128]{3,2,1,0:T(8,128)S(1)} %all-to-all-done.sums_ref, bf16[1,4,4,1408,256]{4,3,2,1,0:T(8,128)(2,1)} %cache_ref.1, ...), custom_call_target="tpu_custom_call" | custom-call | flops 230686720 | bytes 17301504 | tf_op jit(solution)/shard_map/attend/pallas_call | solution.py:310
  39.3 0.1 broadcast_in_dim.6
  39.3 43.8 %all_to_all.10 = bf16[8,2,4096]{2,1,0:T(2,128)(2,1)S(1)} all-to-all(bf16[8,2,4096]{2,1,0:T(2,128)(2,1)S(1)} %broadcast_in_dim.6), channel_id=1, replica_groups={{0,4,8,12,16,20,24,28},{2,6,10,14,18,22,26,30},{1,5,9,13,17,21,25,29},{..., dimensions={0} | all-to-all | bytes 262144 | tf_op jit(solution)/shard_map/all_to_all | solution.py:361
  83.2 0.1 copy.18
  83.3 0.1 collective-permute-start.122
  83.3 1.3 %collective-permute-done.122 = bf16[8,2,4096]{2,0,1:T(8,128)(2,1)S(1)} collective-permute-done((bf16[8,2,4096]{2,0,1:T(8,128)(2,1)S(1)}, bf16[8,2,4096]{2,0,1:T(8,128)(2,1)S(1)}, u32[]{:S(2)}, u32[]{:S(2)}) %collective-permute-start.122) | collective-permute-done | bytes 131104 | tf_op jit(solution)/shard_map/ppermute | solution.py:356
  84.7 0.2 select_bitcast_fusion.1
  84.9 0.3 copy.21
  85.2 0.1 reshape.35
  85.3 3.0 %fusion.2 = f32[32,512]{1,0:T(8,128)S(1)} fusion(bf16[32,4096]{1,0:T(8,128)(2,1)S(1)} %reshape.35, bf16[4096,512]{1,0:T(8,128)(2,1)} %param.144), kind=kOutput, calls=%fused_computation.13 | convolution fusion | flops 134217728 | bytes 4521984 | tf_op jit(solution)/shard_map/dot_general | solution.py:379
  88.3 1.5 %collective-permute-start.123 = (f32[32,512]{1,0:T(8,128)S(1)}, f32[32,512]{1,0:T(8,128)S(1)}, u32[]{:S(2)}, u32[]{:S(2)}) collective-permute-start(f32[32,512]{1,0:T(8,128)S(1)} %fusion.2), channel_id=1, source_target_pairs={{0,1},{1,0},{2,3},{3,2},{4,5},{5,4},{6,7},{7,6},{8,9},{9,8},{10,11... | collective-permute-start | bytes 196616 | tf_op jit(solution)/shard_map/ppermute | solution.py:356
  90.5 2.1 %collective-permute-done.123 = f32[32,512]{1,0:T(8,128)S(1)} collective-permute-done((f32[32,512]{1,0:T(8,128)S(1)}, f32[32,512]{1,0:T(8,128)S(1)}, u32[]{:S(2)}, u32[]{:S(2)}) %collective-permute-start.123) | collective-permute-done | bytes 65568 | tf_op jit(solution)/shard_map/ppermute | solution.py:356
  92.6 0.6 add_convert_fusion
  (14 shorter events, 0.1 us)
Async XLA Ops:
  7.2 16.6 %copy-start.1 = (bf16[1,4,1408,256]{3,2,1,0:T(8,128)(2,1)S(1)}, bf16[1,4,1408,256]{3,2,1,0:T(8,128)(2,1)}, u32[]{:S(2)}) copy-start(bf16[1,4,1408,256]{3,2,1,0:T(8,128)(2,1)} %param.147) | copy-start | bytes 8650756
  7.2 16.6 %copy-start.3 = (s32[2,2,3]{2,1,0:T(2,128)S(1)}, s32[2,2,3]{2,1,0:T(2,128)}, u32[]{:S(2)}) copy-start(s32[2,2,3]{2,1,0:T(2,128)} %join_ref.1) | copy-start | bytes 148
  7.2 15.8 %copy-start.4 = (s32[2,1]{0,1:T(1,128)S(1)}, s32[2,1]{0,1:T(1,128)}, u32[]{:S(2)}) copy-start(s32[2,1]{0,1:T(1,128)} %param.148) | copy-start | bytes 28
  7.2 16.5 %collective-permute-start.121 = (bf16[4,1408,256]{2,1,0:T(8,128)(2,1)}, bf16[4,1408,256]{2,1,0:T(8,128)(2,1)}, u32[]{:S(2)}, u32[]{:S(2)}) collective-permute-start(bf16[4,1408,256]{2,1,0:T(8,128)(2,1)} %bitcast.29), channel_id=1, source_target_pairs={{0,2},{2,0},{4,6},{6,4},{8,10},{10,8},{12,14},{14,12},{16,18},{18,... | collective-permute-start | bytes 8650760 | tf_op jit(solution)/shard_map/ppermute | solution.py:356
  12.8 1.7 %collective-permute-start.120 = (f32[8,2,32,128]{3,2,1,0:T(8,128)}, f32[8,2,32,128]{3,2,1,0:T(8,128)S(1)}, u32[]{:S(2)}, u32[]{:S(2)}) collective-permute-start(f32[8,2,32,128]{3,2,1,0:T(8,128)} %get-tuple-element.293), channel_id=1, source_target_pairs={{0,2},{2,0},{4,6},{6,4},{8,10},{10,8},{12,14},{14,12},{16,18},{18,... | collective-permute-start | bytes 786440 | tf_op jit(solution)/shard_map/ppermute | solution.py:356
  16.2 16.2 %all-to-all-start = ((f32[8,2,32,128]{3,2,1,0:T(8,128)}), f32[8,2,32,128]{3,2,1,0:T(8,128)S(1)}, u32[]{:S(2)}, u32[]{:S(2)}) async-start(f32[8,2,32,128]{3,2,1,0:T(8,128)} %add.17), calls=%async_computation | async-start | bytes 524288 | tf_op jit(solution)/shard_map/all_to_all | solution.py:361
  23.8 8.7 %copy-start = (bf16[128]{0:T(256)(128)(2,1)S(1)}, bf16[128]{0:T(256)(128)(2,1)}, u32[]{:S(2)}) copy-start(bf16[128]{0:T(256)(128)(2,1)} %param.143) | copy-start | bytes 772
  83.3 1.4 %collective-permute-start.122 = (bf16[8,2,4096]{2,0,1:T(8,128)(2,1)S(1)}, bf16[8,2,4096]{2,0,1:T(8,128)(2,1)S(1)}, u32[]{:S(2)}, u32[]{:S(2)}) collective-permute-start(bf16[8,2,4096]{2,0,1:T(8,128)(2,1)S(1)} %copy.18), channel_id=1, source_target_pairs={{0,2},{2,0},{4,6},{6,4},{8,10},{10,8},{12,14},{14,12},{16,18},{18,... | collective-permute-start | bytes 393224 | tf_op jit(solution)/shard_map/ppermute | solution.py:356
  84.9 7.7 %copy-start.2 = (bf16[2,16,512]{2,1,0:T(8,128)(2,1)S(1)}, bf16[2,16,512]{2,1,0:T(8,128)(2,1)}, u32[]{:S(2)}) copy-start(bf16[2,16,512]{2,1,0:T(8,128)(2,1)} %param.140) | copy-start | bytes 98308
  88.3 4.3 %collective-permute-start.123 = (f32[32,512]{1,0:T(8,128)S(1)}, f32[32,512]{1,0:T(8,128)S(1)}, u32[]{:S(2)}, u32[]{:S(2)}) collective-permute-start(f32[32,512]{1,0:T(8,128)S(1)} %fusion.2), channel_id=1, source_target_pairs={{0,1},{1,0},{2,3},{3,2},{4,5},{5,4},{6,7},{7,6},{8,9},{9,8},{10,11... | collective-permute-start | bytes 196616 | tf_op jit(solution)/shard_map/ppermute | solution.py:356
where the time goes:
time: 100 us
  blocking collectives  43.8 us (44%)
  between operations  15.5 us (16%)
  Pallas kernels  11.9 us (12%)
  waiting for transfers between devices  11.3 us (11%)
  starting transfers between devices  8.91 us (9%)
  matrix products  3 us (3%)
  other arithmetic  2.5 us (2%)
  local copies, waits for them, and re-layouts  2.41 us (2%)
    all_to_all x1, blocking collectives, between_chips(): lax.all_to_all(blocks, 'rows', 0, 0, axis_index_groups=same_core, tiled=T...  43.8 us
    all_to_all x1, starting transfers between devices, between_chips(): lax.all_to_all(blocks, 'rows', 0, 0, axis_index_groups=same_core, tiled=T...  6.79 us
    pallas_call x1, Pallas kernels, attend(): pl.pallas_call(functools.partial(attend_kernel, group, head_size), in_spe...  6.78 us
    all_to_all x1, waiting for transfers between devices, between_chips(): lax.all_to_all(blocks, 'rows', 0, 0, axis_index_groups=same_core, tiled=T...  6.21 us
    ppermute x4, waiting for transfers between devices, across(): return lax.ppermute(block, axis, [(i, i ^ key) for i in range(size)])  5.13 us
    pallas_call x1, Pallas kernels, project(): pl.pallas_call(functools.partial(project_kernel, rows, head_size), grid=(...  5.07 us
    dot_general x1, matrix products, on_device(): jnp.dot(gathered, out_weight, preferred_element_type=jnp.float32)  3 us
    ppermute x4, starting transfers between devices, across(): return lax.ppermute(block, axis, [(i, i ^ key) for i in range(size)])  2.13 us
  transfers between devices with their start and end apart: 5, of which 4 were waited for; matrix products, arithmetic and copies ran while one was open for 4% of the time, Pallas kernels for 5%

commit v1 on v0

--- a/solution.py
+++ b/solution.py
@@ -18,7 +18,7 @@
           (0, 1, 1, 0), (0, 1, 0, 1), (0, 0, 1, 1), (0, 1, 1, 1)]
 
 
-def write_plan(rows, join_ref, only_ref, way_ref, plan_ref):
+def write_plan(rows, join_ref, only_ref, plan_ref):
     me = lax.axis_index("rows")
     source, target, slot = [], [], []
     for s in range(STEPS):
@@ -89,8 +89,9 @@
         arrives = jnp.where(here, best[i] + 1, arrives)
         step = jnp.where(here, i // JOINS, step)
         place = jnp.where(here, slot[i], place)
-    only_ref[0] = only
-    way_ref[0] = jnp.where(single > 0, 0, jnp.where(double > 0, 1, 2))
+    rest = 1 + 2 * (2 * rows - 1)
+    rest = jnp.where(double > 0, jnp.int32(rest), jnp.int32(rest + 1))
+    only_ref[0] = jnp.where(single > 0, only, rest)
     plan_ref[0] = branch[0]
     plan_ref[1] = branch[1]
     plan_ref[2] = arrives
@@ -101,72 +102,130 @@
 
 
 def project_kernel(
-    rows, head_size, join_ref, hidden_ref, gain_ref, weight_ref,
-    keep_ref, send_ref, only_ref, way_ref, plan_ref, scaled_ref,
+    rows, head_size, parts, join_ref, hidden_ref, gain_ref, weight_ref,
+    keep_ref, send_ref, only_ref, plan_ref, held, hidden, gain, sem, small_sem,
 ):
     chips = rows // 2
-
-    @pl.when(pl.program_id(0) == 0)
-    def _():
-        write_plan(rows, join_ref, only_ref, way_ref, plan_ref)
-        scaled = hidden_ref[...].astype(jnp.float32) * gain_ref[...].astype(jnp.float32)[None, :]
-        scaled = scaled.astype(jnp.bfloat16)
-        count = STEPS * rows
-        to = lax.broadcasted_iota(jnp.int32, (count, count), 0)
-        given = lax.broadcasted_iota(jnp.int32, (count, count), 1)
-        core = (to // (STEPS * chips)) ^ (lax.axis_index("rows") & 1)
-        wanted = lax.rem(to // chips, STEPS) * rows + lax.rem(to, chips) * 2 + core
-        shuffle = jnp.where(given == wanted, 1.0, 0.0).astype(jnp.bfloat16)
-        scaled_ref[...] = jnp.dot(
-            shuffle, scaled, preferred_element_type=jnp.float32
-        ).astype(jnp.bfloat16)
-
-    product = jnp.dot(scaled_ref[...], weight_ref[...], preferred_element_type=jnp.float32)
-    for h in range(weight_ref.shape[1] // head_size):
-        piece = product[:, h * head_size:(h + 1) * head_size]
-        for s in range(STEPS):
-            keep_ref[:, s, h, :] = piece[s * chips:(s + 1) * chips]
-            start = (STEPS + s) * chips
-            send_ref[:, s, h, :] = piece[start:start + chips]
+    wide = weight_ref.shape[1] // parts
+    fetches = [
+        pltpu.make_async_copy(
+            weight_ref.at[:, pl.ds(i * wide, wide)], held.at[i], sem.at[i]
+        )
+        for i in range(parts)
+    ]
+    small = [
+        pltpu.make_async_copy(hidden_ref, hidden, small_sem.at[0]),
+        pltpu.make_async_copy(gain_ref, gain, small_sem.at[1]),
+    ]
+    for fetch in small + fetches:
+        fetch.start()
+    write_plan(rows, join_ref, only_ref, plan_ref)
+    for fetch in small:
+        fetch.wait()
+    scaled = hidden[...].astype(jnp.float32) * gain[...].astype(jnp.float32)[None, :]
+    scaled = scaled.astype(jnp.bfloat16)
+    count = STEPS * rows
+    to = lax.broadcasted_iota(jnp.int32, (count, count), 0)
+    given = lax.broadcasted_iota(jnp.int32, (count, count), 1)
+    core = (to // (STEPS * chips)) ^ (lax.axis_index("rows") & 1)
+    wanted = lax.rem(to // chips, STEPS) * rows + lax.rem(to, chips) * 2 + core
+    shuffle = jnp.where(given == wanted, 1.0, 0.0).astype(jnp.bfloat16)
+    scaled = jnp.dot(shuffle, scaled, preferred_element_type=jnp.float32).astype(jnp.bfloat16)
+    for i in range(parts):
+        fetches[i].wait()
+        product = jnp.dot(scaled, held[i], preferred_element_type=jnp.float32)
+        for j in range(wide // head_size):
+            h = i * (wide // head_size) + j
+            piece = product[:, j * head_size:(j + 1) * head_size]
+            for s in range(STEPS):
+                keep_ref[:, s, h, :] = piece[s * chips:(s + 1) * chips]
+                start = (STEPS + s) * chips
+                send_ref[:, s, h, :] = piece[start:start + chips]
 
 
 def project(rows, head_size, join_list, hidden, norm_gain, query_weight):
     width, columns = query_weight.shape
     chips = rows // 2
     heads_here = columns // head_size
-    parts = 4 if heads_here % 32 == 0 else 1
+    parts = min(2, heads_here)
     smem = pl.BlockSpec(memory_space=pltpu.SMEM)
-    block = pl.BlockSpec((chips, STEPS, heads_here // parts, head_size), lambda i: (0, 0, i, 0))
+    vmem = pl.BlockSpec(memory_space=pltpu.VMEM)
+    hbm = pl.BlockSpec(memory_space=pltpu.HBM)
+    pinned = [
+        pltpu.with_memory_space_constraint(x, pltpu.HBM)
+        for x in (hidden.reshape(STEPS * rows, width), norm_gain, query_weight)
+    ]
     sums = jax.ShapeDtypeStruct((chips, STEPS, heads_here, head_size), jnp.float32)
     return pl.pallas_call(
-        functools.partial(project_kernel, rows, head_size),
-        grid=(parts,),
+        functools.partial(project_kernel, rows, head_size, parts),
         out_shape=(
             sums,
             sums,
             jax.ShapeDtypeStruct((1,), jnp.int32),
-            jax.ShapeDtypeStruct((1,), jnp.int32),
             jax.ShapeDtypeStruct((8,), jnp.int32),
         ),
-        in_specs=[
-            smem,
-            pl.BlockSpec((STEPS * rows, width), lambda i: (0, 0)),
-            pl.BlockSpec((width,), lambda i: (0,)),
-            pl.BlockSpec((width, columns // parts), lambda i: (0, i)),
+        in_specs=[smem, hbm, hbm, hbm],
+        out_specs=(vmem, vmem, smem, smem),
+        scratch_shapes=[
+            pltpu.VMEM((parts, width, columns // parts), jnp.bfloat16),
+            pltpu.VMEM((STEPS * rows, width), jnp.bfloat16),
+            pltpu.VMEM((width,), jnp.bfloat16),
+            pltpu.SemaphoreType.DMA((parts,)),
+            pltpu.SemaphoreType.DMA((2,)),
         ],
-        out_specs=(block, block, smem, smem, smem),
-        scratch_shapes=[pltpu.VMEM((STEPS * rows, width), jnp.bfloat16)],
-        compiler_params=pltpu.CompilerParams(vmem_limit_bytes=60 * 1024 * 1024),
+        compiler_params=pltpu.CompilerParams(vmem_limit_bytes=24 * 1024 * 1024),
         cost_estimate=pl.CostEstimate(
             flops=2 * STEPS * rows * width * columns,
             bytes_accessed=2 * width * columns + 4 * STEPS * rows * columns,
             transcendentals=0,
         ),
         name="project",
-    )(join_list, hidden.reshape(STEPS * rows, width), norm_gain, query_weight)
-
-
-def transfer(branch, rows, *tiles):
+    )(join_list, *pinned)
+
+
+def output_kernel(parts, context_ref, weight_ref, out_ref, held, sem):
+    deep = weight_ref.shape[0] // parts
+    fetches = [
+        pltpu.make_async_copy(weight_ref.at[pl.ds(i * deep, deep)], held.at[i], sem.at[i])
+        for i in range(parts)
+    ]
+    for fetch in fetches:
+        fetch.start()
+    total = jnp.zeros(out_ref.shape, jnp.float32)
+    for i in range(parts):
+        fetches[i].wait()
+        total = total + jnp.dot(
+            context_ref[:, i * deep:(i + 1) * deep],
+            held[i],
+            preferred_element_type=jnp.float32,
+        )
+    out_ref[...] = total
+
+
+def output(context, out_weight):
+    deep, width = out_weight.shape
+    parts = 8
+    vmem = pl.BlockSpec(memory_space=pltpu.VMEM)
+    return pl.pallas_call(
+        functools.partial(output_kernel, parts),
+        out_shape=jax.ShapeDtypeStruct((context.shape[0], width), jnp.float32),
+        in_specs=[vmem, pl.BlockSpec(memory_space=pltpu.HBM)],
+        out_specs=vmem,
+        scratch_shapes=[
+            pltpu.VMEM((parts, deep // parts, width), jnp.bfloat16),
+            pltpu.SemaphoreType.DMA((parts,)),
+        ],
+        compiler_params=pltpu.CompilerParams(vmem_limit_bytes=24 * 1024 * 1024),
+        cost_estimate=pl.CostEstimate(
+            flops=2 * context.size * width,
+            bytes_accessed=2 * deep * width + 2 * context.size,
+            transcendentals=0,
+        ),
+        name="output",
+    )(context, pltpu.with_memory_space_constraint(out_weight, pltpu.HBM))
+
+
+def transfer(branch, rows, tiles, others=()):
     branches = [lambda *blocks: jnp.zeros_like(blocks[0])]
 
     def keep(index):
@@ -181,18 +240,15 @@
             for low in (True, False):
                 pairs = [(i, i ^ key) for i in range(rows) if (i < (i ^ key)) == low]
                 branches.append(send(index, pairs))
-    return lax.switch(branch, branches, *tiles)
-
-
-def move_tiles(only, way, plan, join_list, rows, own, other):
+    return lax.switch(branch, branches + list(others), *tiles)
+
+
+def move_tiles(only, plan, join_list, rows, own, other):
     me = lax.axis_index("rows")
 
-    def once(own, other):
-        return transfer(only[0], rows, own, other)
-
     def twice(own, other):
-        first = transfer(plan[0], rows, own)
-        second = transfer(plan[1], rows, own)
+        first = transfer(plan[0], rows, (own,))
+        second = transfer(plan[1], rows, (own,))
         late = plan[2] == 2
         return jnp.where(plan[2] == 1, first, jnp.where(late, second, jnp.zeros_like(own)))
 
@@ -205,7 +261,7 @@
                 result = jnp.where(me == join_list[s, j, 1], given, result)
         return result
 
-    return lax.switch(way[0], [once, twice, summed], own, other)
+    return transfer(only[0], rows, (own, other), (twice, summed))
 
 
 def attend_kernel(
@@ -306,7 +362,8 @@
     group = heads_here // kv_here
     smem = pl.BlockSpec(memory_space=pltpu.SMEM)
     vmem = pl.BlockSpec(memory_space=pltpu.VMEM)
-    hbm = pl.BlockSpec(memory_space=pl.ANY)
+    hbm = pl.BlockSpec(memory_space=pltpu.HBM)
+    pinned = [pltpu.with_memory_space_constraint(x, pltpu.HBM) for x in (kv_cache, arrived)]
     return pl.pallas_call(
         functools.partial(attend_kernel, group, head_size),
         in_specs=[smem, smem, vmem, vmem, hbm, hbm],
@@ -322,14 +379,14 @@
             pltpu.SemaphoreType.DMA((kv_here,)),
             pltpu.SemaphoreType.DMA((kv_here,)),
         ],
-        compiler_params=pltpu.CompilerParams(vmem_limit_bytes=53 * 1024 * 1024),
+        compiler_params=pltpu.CompilerParams(vmem_limit_bytes=40 * 1024 * 1024),
         cost_estimate=pl.CostEstimate(
             flops=4 * kv_here * (slots + 1) * tile_len * width * group,
             bytes_accessed=kv_here * (slots + 2) * tile_len * width * 2,
             transcendentals=kv_here * (slots + 1) * tile_len * group * STEPS,
         ),
         name="attend",
-    )(plan, counts, query_gain.reshape(1, head_size), sums, kv_cache, arrived)
+    )(plan, counts, query_gain.reshape(1, head_size), sums, *pinned)
 
 
 def on_device(
@@ -363,11 +420,11 @@
     other_tile = across(own_tile, "rows", rows, 1)
     head_size = kv_cache.shape[4] // 2
     columns = query_weight.shape[1]
-    keep, send, only, way, plan = project(
+    keep, send, only, plan = project(
         rows, head_size, join_list, hidden, norm_gain, query_weight
     )
     sums = between_chips(keep + across(send, "rows", rows, 1))
-    arrived = move_tiles(only, way, plan, join_list, rows, own_tile, other_tile)
+    arrived = move_tiles(only, plan, join_list, rows, own_tile, other_tile)
     context, arrived = attend(plan, counts, query_gain, sums, kv_cache, arrived)
     context = context.astype(jnp.bfloat16)
     mine = between_chips(jnp.broadcast_to(context, (chips, STEPS, columns)))
@@ -376,7 +433,7 @@
         [jnp.where(odd, theirs, mine), jnp.where(odd, mine, theirs)], axis=1
     )
     gathered = gathered.transpose(2, 0, 1, 3).reshape(STEPS * rows, columns)
-    projected = jnp.dot(gathered, out_weight, preferred_element_type=jnp.float32)
+    projected = output(gathered, out_weight)
     key = 1
     while key < heads:
         projected = projected + across(projected, "heads", heads, key)

time: 100 us -> 127 us (1.27)
  blocking collectives: 43.8 us -> 74.6 us
  matrix products: 3 us -> 0 us
    all_to_all x1, blocking collectives: 43.8 us -> 74.6 us  [between_chips(): lax.all_to_all(blocks, 'rows', 0, 0, axis_index_groups=same_core, tiled=T...]
    dot_general x1 -> x0, matrix products: 3 us -> none  [on_device(): jnp.dot(gathered, out_weight, preferred_element_type=jnp.float32)]
    pallas_call x1 -> x2, Pallas kernels: 5.07 us -> 6.13 us  [the longest x1 3.72 us: project(): pl.pallas_call(functools.partial(project_kernel, rows, head_size, parts),...]
  transfers between devices with their start and end apart: 5 -> 5, of which waited for: 4 -> 4; matrix products, arithmetic and copies ran while one was open for 4% -> 2% of each run, Pallas kernels for 5% -> 3%
where the time goes in v1:
time: 127 us; the launch traced here: 128 us
  blocking collectives  74.6 us (59%)
  between operations  15.5 us (12%)
  Pallas kernels  12.9 us (10%)
  waiting for transfers between devices  11.5 us (9%)
  starting transfers between devices  9.43 us (7%)
  local copies, waits for them, and re-layouts  2.41 us (2%)
  other arithmetic  1.58 us (1%)
    all_to_all x1, blocking collectives, between_chips(): lax.all_to_all(blocks, 'rows', 0, 0, axis_index_groups=same_core, tiled=T...  74.6 us
    all_to_all x1, starting transfers between devices, between_chips(): lax.all_to_all(blocks, 'rows', 0, 0, axis_index_groups=same_core, tiled=T...  7.13 us
    pallas_call x1, Pallas kernels, attend(): pl.pallas_call(functools.partial(attend_kernel, group, head_size), in_spe...  6.78 us
    all_to_all x1, waiting for transfers between devices, between_chips(): lax.all_to_all(blocks, 'rows', 0, 0, axis_index_groups=same_core, tiled=T...  6.66 us
    ppermute x4, waiting for transfers between devices, across(): return lax.ppermute(block, axis, [(i, i ^ key) for i in range(size)])  4.87 us
    pallas_call x1, Pallas kernels, project(): pl.pallas_call(functools.partial(project_kernel, rows, head_size, parts),...  3.72 us
  transfers between devices with their start and end apart: 5, of which 4 were waited for; matrix products, arithmetic and copies ran while one was open for 2% of the time, Pallas kernels for 3%

profile of v1, /device:TPU:0, one launch (start us, length us, event | category | flops | bytes accessed | tf_op | source)
XLA Modules:
  0.0 128.0 jit_solution(4342450190708104969)
XLA Ops:
  7.2 0.5 collective-permute-start.121
  7.7 3.7 %project.1 = (f32[8,2,32,128]{3,2,1,0:T(8,128)S(1)}, f32[8,2,32,128]{3,2,1,0:T(8,128)S(1)}, s32[1]{0:T(128)}, s32[8]{0:T(128)S(1)}) custom-call(s32[2,2,3]{2,1,0:T(2,128)} %join_ref.1, bf16[32,512]{1,0:T(8,128)(2,1)} %bitcast.61, bf16[512]{0:T(512)(128)(2,1)} %gain_ref.1, bf16[512,4096]{1,0:T(8,128)(2,1)} %weight_ref.2), custom_call_target="tpu_custom_call" | custom-call | flops 134217728 | bytes 4718592 | tf_op jit(solution)/shard_map/project/pallas_call | solution.py:159
  11.4 0.1 collective-permute-start.120
  11.6 1.5 %collective-permute-done.120 = f32[8,2,32,128]{3,2,1,0:T(8,128)S(1)} collective-permute-done((f32[8,2,32,128]{3,2,1,0:T(8,128)S(1)}, f32[8,2,32,128]{3,2,1,0:T(8,128)S(1)}, u32[]{:S(2)}, u32[]{:S(2)}) %collective-permute-start.120) | collective-permute-done | bytes 262176 | tf_op jit(solution)/shard_map/ppermute | solution.py:413
  13.0 0.7 add.17
  13.8 7.1 %all-to-all-start = ((f32[8,2,32,128]{3,2,1,0:T(8,128)}), f32[8,2,32,128]{3,2,1,0:T(8,128)S(1)}, u32[]{:S(2)}, u32[]{:S(2)}) async-start(f32[8,2,32,128]{3,2,1,0:T(8,128)} %add.17), calls=%async_computation | async-start | bytes 524288 | tf_op jit(solution)/shard_map/all_to_all | solution.py:418
  20.9 0.1 copy.16.counts_ref
  21.7 0.0 copy-start
  21.7 1.8 %conditional.3 = (bf16[4,1408,256]{2,1,0:T(8,128)(2,1)}) conditional(s32[]{:T(128)} %bitcast.15, () %tuple.395, bf16[4,1408,256]{2,1,0:T(8,128)(2,1)S(1)} %bitcast.42, bf16[4,1408,256]{2,1,0:T(8,128)(2,1)S(1)} %bitcast.59, bf16[4,1408,256]{2,1,0:T(8,128)(2,1)S(1)} %bitcast.29, ...), branch_computations={%region_0.0_spmd, %region_1.0_spmd, %region_2.0_spmd, %region_3.0_... | conditional | flops 17301512 | bytes 98042040 | solution.py:243
  21.8 1.8 %broadcast.12 = bf16[4,1408,256]{2,1,0:T(8,128)(2,1)} broadcast(bf16[]{:T(256)} %constant.11.clone), dimensions={} | broadcast | bytes 2883586 | tf_op jit(solution)/shard_map/broadcast.1
  23.5 6.7 %all-to-all-done.sums_ref = f32[8,2,32,128]{3,2,1,0:T(8,128)S(1)} async-done(((f32[8,2,32,128]{3,2,1,0:T(8,128)}), f32[8,2,32,128]{3,2,1,0:T(8,128)S(1)}, u32[]{:S(2)}, u32[]{:S(2)}) %all-to-all-start) | async-done | bytes 262176 | tf_op jit(solution)/shard_map/all_to_all | solution.py:418
  30.2 6.8 %attend.1 = (f32[2,4096]{1,0:T(2,128)S(1)}, bf16[4,1408,256]{2,1,0:T(8,128)(2,1)}) custom-call(s32[8]{0:T(128)S(1)} %get-tuple-element.279.plan_ref, s32[2,1]{1,0:T(2,128)S(1)} %copy.16.counts_ref, bf16[1,128]{1,0:T(2,128)(2,1)S(1)} %bitcast.25, f32[8,2,32,128]{3,2,1,0:T(8,128)S(1)} %all-to-all-done.sums_ref, bf16[1,4,4,1408,256]{4,3,2,1,0:T(8,128)(2,1)} %cache_ref.1, ...), custom_call_target="tpu_custom_call" | custom-call | flops 230686720 | bytes 17301504 | tf_op jit(solution)/shard_map/attend/pallas_call | solution.py:367
  37.0 0.1 broadcast_in_dim.6
  37.1 74.6 %all_to_all.10 = bf16[8,2,4096]{2,1,0:T(2,128)(2,1)S(1)} all-to-all(bf16[8,2,4096]{2,1,0:T(2,128)(2,1)S(1)} %broadcast_in_dim.6), channel_id=1, replica_groups={{0,4,8,12,16,20,24,28},{2,6,10,14,18,22,26,30},{1,5,9,13,17,21,25,29},{..., dimensions={0} | all-to-all | bytes 262144 | tf_op jit(solution)/shard_map/all_to_all | solution.py:418
  111.7 0.1 copy.17
  111.8 0.1 collective-permute-start.122
  111.9 1.3 %collective-permute-done.122 = bf16[8,2,4096]{2,0,1:T(8,128)(2,1)S(1)} collective-permute-done((bf16[8,2,4096]{2,0,1:T(8,128)(2,1)S(1)}, bf16[8,2,4096]{2,0,1:T(8,128)(2,1)S(1)}, u32[]{:S(2)}, u32[]{:S(2)}) %collective-permute-start.122) | collective-permute-done | bytes 131104 | tf_op jit(solution)/shard_map/ppermute | solution.py:413
  113.2 0.2 select_bitcast_fusion.1
  113.4 0.3 copy.20
  113.7 0.1 reshape.32.context_ref
  113.8 2.4 %output.1 = f32[32,512]{1,0:T(8,128)S(1)} custom-call(bf16[32,4096]{1,0:T(8,128)(2,1)S(1)} %reshape.32.context_ref, bf16[4096,512]{1,0:T(8,128)(2,1)} %weight_ref.3), custom_call_target="tpu_custom_call" | custom-call | flops 134217728 | bytes 4456448 | tf_op jit(solution)/shard_map/output/pallas_call | solution.py:209
  116.2 1.6 %collective-permute-start.123 = (f32[32,512]{1,0:T(8,128)S(1)}, f32[32,512]{1,0:T(8,128)S(1)}, u32[]{:S(2)}, u32[]{:S(2)}) collective-permute-start(f32[32,512]{1,0:T(8,128)S(1)} %output.1), channel_id=1, source_target_pairs={{0,1},{1,0},{2,3},{3,2},{4,5},{5,4},{6,7},{7,6},{8,9},{9,8},{10,11... | collective-permute-start | bytes 196616 | tf_op jit(solution)/shard_map/ppermute | solution.py:413
  118.5 2.1 %collective-permute-done.123 = f32[32,512]{1,0:T(8,128)S(1)} collective-permute-done((f32[32,512]{1,0:T(8,128)S(1)}, f32[32,512]{1,0:T(8,128)S(1)}, u32[]{:S(2)}, u32[]{:S(2)}) %collective-permute-start.123) | collective-permute-done | bytes 65568 | tf_op jit(solution)/shard_map/ppermute | solution.py:413
  120.6 0.6 add_convert_fusion
  (13 shorter events, 0.1 us)
Async XLA Ops:
  7.2 14.5 %copy-start.1 = (bf16[1,4,1408,256]{3,2,1,0:T(8,128)(2,1)S(1)}, bf16[1,4,1408,256]{3,2,1,0:T(8,128)(2,1)}, u32[]{:S(2)}) copy-start(bf16[1,4,1408,256]{3,2,1,0:T(8,128)(2,1)} %param.146) | copy-start | bytes 8650756
  7.2 14.5 %copy-start.3 = (s32[2,2,3]{2,1,0:T(2,128)S(1)}, s32[2,2,3]{2,1,0:T(2,128)}, u32[]{:S(2)}) copy-start(s32[2,2,3]{2,1,0:T(2,128)} %join_ref.1) | copy-start | bytes 148
  7.2 13.7 %copy-start.4 = (s32[2,1]{0,1:T(1,128)S(1)}, s32[2,1]{0,1:T(1,128)}, u32[]{:S(2)}) copy-start(s32[2,1]{0,1:T(1,128)} %param.147) | copy-start | bytes 28
  7.2 14.5 %collective-permute-start.121 = (bf16[4,1408,256]{2,1,0:T(8,128)(2,1)}, bf16[4,1408,256]{2,1,0:T(8,128)(2,1)}, u32[]{:S(2)}, u32[]{:S(2)}) collective-permute-start(bf16[4,1408,256]{2,1,0:T(8,128)(2,1)} %bitcast.26), channel_id=1, source_target_pairs={{0,2},{2,0},{4,6},{6,4},{8,10},{10,8},{12,14},{14,12},{16,18},{18,... | collective-permute-start | bytes 8650760 | tf_op jit(solution)/shard_map/ppermute | solution.py:413
  11.4 1.6 %collective-permute-start.120 = (f32[8,2,32,128]{3,2,1,0:T(8,128)S(1)}, f32[8,2,32,128]{3,2,1,0:T(8,128)S(1)}, u32[]{:S(2)}, u32[]{:S(2)}) collective-permute-start(f32[8,2,32,128]{3,2,1,0:T(8,128)S(1)} %get-tuple-element.281), channel_id=1, source_target_pairs={{0,2},{2,0},{4,6},{6,4},{8,10},{10,8},{12,14},{14,12},{16,18},{18,... | collective-permute-start | bytes 786440 | tf_op jit(solution)/shard_map/ppermute | solution.py:413
  13.8 16.4 %all-to-all-start = ((f32[8,2,32,128]{3,2,1,0:T(8,128)}), f32[8,2,32,128]{3,2,1,0:T(8,128)S(1)}, u32[]{:S(2)}, u32[]{:S(2)}) async-start(f32[8,2,32,128]{3,2,1,0:T(8,128)} %add.17), calls=%async_computation | async-start | bytes 524288 | tf_op jit(solution)/shard_map/all_to_all | solution.py:418
  21.7 8.5 %copy-start = (bf16[128]{0:T(256)(128)(2,1)S(1)}, bf16[128]{0:T(256)(128)(2,1)}, u32[]{:S(2)}) copy-start(bf16[128]{0:T(256)(128)(2,1)} %param.142) | copy-start | bytes 772
  111.8 1.4 %collective-permute-start.122 = (bf16[8,2,4096]{2,0,1:T(8,128)(2,1)S(1)}, bf16[8,2,4096]{2,0,1:T(8,128)(2,1)S(1)}, u32[]{:S(2)}, u32[]{:S(2)}) collective-permute-start(bf16[8,2,4096]{2,0,1:T(8,128)(2,1)S(1)} %copy.17), channel_id=1, source_target_pairs={{0,2},{2,0},{4,6},{6,4},{8,10},{10,8},{12,14},{14,12},{16,18},{18,... | collective-permute-start | bytes 393224 | tf_op jit(solution)/shard_map/ppermute | solution.py:413
  113.4 7.2 %copy-start.2 = (bf16[2,16,512]{2,1,0:T(8,128)(2,1)S(1)}, bf16[2,16,512]{2,1,0:T(8,128)(2,1)}, u32[]{:S(2)}) copy-start(bf16[2,16,512]{2,1,0:T(8,128)(2,1)} %param.139) | copy-start | bytes 98308
  116.2 4.3 %collective-permute-start.123 = (f32[32,512]{1,0:T(8,128)S(1)}, f32[32,512]{1,0:T(8,128)S(1)}, u32[]{:S(2)}, u32[]{:S(2)}) collective-permute-start(f32[32,512]{1,0:T(8,128)S(1)} %output.1), channel_id=1, source_target_pairs={{0,1},{1,0},{2,3},{3,2},{4,5},{5,4},{6,7},{7,6},{8,9},{9,8},{10,11... | collective-permute-start | bytes 196616 | tf_op jit(solution)/shard_map/ppermute | solution.py:413
